TPU v7x, 512 devices: a whole 4x4x16 slice. The times are simulated.
512 devices in a mesh: blk: 32 (over x_lo, z), resp: 4 (over x_hi, core), batch: 4 (over y).
Axes of the slice: x: 4 (x_hi: 2, x_lo: 2; x = x_hi * 2 + x_lo), y: 4, z: 16, core: 2. Of those that a mesh axis runs over, the one named last changes fastest.
Arguments:
- prompt_query: bfloat16 [12288, 512], P(('batch', 'blk'), 'resp'), parts along dimension 0, may hold values from -22 to 22
- answer_query: bfloat16 [8, 2048, 512], P('batch', 'blk', 'resp'), parts along dimension 0, may hold values from -22 to 22
- prompt_kv: bfloat16 [12288, 256], P(('batch', 'blk')), parts along dimension 0, may hold values from -5 to 5
- answer_kv: bfloat16 [8, 2048, 256], P('batch', 'blk'), parts along dimension 0, may hold values from -5 to 5
- prompt_grad: bfloat16 [12288, 512], P(('batch', 'blk'), 'resp'), parts along dimension 0, may hold values from -6 to 6
- answer_grad: bfloat16 [8, 2048, 512], P('batch', 'blk', 'resp'), parts along dimension 0, may hold values from -6 to 6
- lengths: int32 [12], P('batch'), parts along dimension 0, may hold values from 512 to 3072, as said below
Outputs:
- prompt_out: bfloat16 [12288, 512], P(('batch', 'blk'), 'resp'), parts along dimension 0
- answer_out: bfloat16 [8, 2048, 512], P('batch', 'blk', 'resp'), parts along dimension 0
- prompt_query_grad: bfloat16 [12288, 512], P(('batch', 'blk'), 'resp'), parts along dimension 0
- answer_query_grad: bfloat16 [8, 2048, 512], P('batch', 'blk', 'resp'), parts along dimension 0
- prompt_kv_grad: bfloat16 [12288, 256], P(('batch', 'blk')), parts along dimension 0
- answer_kv_grad: bfloat16 [8, 2048, 256], P('batch', 'blk'), parts along dimension 0
There are 4 independent parts, one for each index of `batch`. A program takes and returns all parts, laid end to end along the dimension named above; each array names one. Nothing has to cross between parts.
Inputs may be any that keep to these rules, and one draw needn't show every extreme that they name: lengths[0] is the prompt's length and equals 3072; lengths[1] and lengths[2] lie from 512 to 2048, and one of them is exactly 2048.
All inputs are finite; a program needn't handle non-finite values.
Results may differ from a plain program's by a relative error of at most 0.005.
Values may be sent and summed in bfloat16 or wider, within the bound.
A program may use at most 64 MiB of HBM per device.

v0:
```python
import math

import jax
import jax.numpy as jnp
from jax import lax
from jax.sharding import PartitionSpec as P


def row_labels(first_row, count, prompt_rows, answer_rows):
    block_rows = prompt_rows + 2 * answer_rows
    indices = first_row + jnp.arange(count, dtype=jnp.int32)
    shard = indices // block_rows
    within = indices - shard * block_rows
    kinds = (within >= prompt_rows).astype(jnp.int32) + (
        within >= prompt_rows + answer_rows
    ).astype(jnp.int32)
    answer_place = (
        shard * answer_rows + within - prompt_rows - jnp.where(kinds == 2, answer_rows, 0)
    )
    places = jnp.where(kinds == 0, shard * prompt_rows + within, answer_place)
    return (kinds, places)


def live_bound(kinds, lengths):
    return jnp.where(kinds == 0, lengths[0], jnp.where(kinds == 1, lengths[1], lengths[2]))


def visible(query_kinds, query_places, key_kinds, key_places, lengths):
    live = (key_places < live_bound(key_kinds, lengths))[None, :]
    causal = key_places[None, :] <= query_places[:, None]
    prompt_key = key_kinds[None, :] == 0
    own_key = (key_kinds[None, :] == query_kinds[:, None]) & (query_kinds[:, None] != 0)
    return live & (prompt_key & ((query_kinds[:, None] != 0) | causal) | own_key & causal)


def contract_last(left, right):
    return lax.dot_general(
        left, right, (((1,), (1,)), ((), ())), preferred_element_type=jnp.float32
    )


def contract_first(left, right):
    return lax.dot_general(
        left, right, (((0,), (0,)), ((), ())), preferred_element_type=jnp.float32
    )


def body(prompt_query, answer_query, prompt_kv, answer_kv, prompt_grad, answer_grad, lengths):
    prompt_rows = prompt_query.shape[0]
    answer_rows = answer_query.shape[1]
    head_dim = prompt_query.shape[1]
    block_rows = prompt_rows + 2 * answer_rows
    scaling = 1.0 / math.sqrt(head_dim)
    block_index = lax.axis_index("blk")
    queries = jnp.concatenate([prompt_query, answer_query[0], answer_query[1]], axis=0)
    cotangent = jnp.concatenate([prompt_grad, answer_grad[0], answer_grad[1]], axis=0)
    key_values = jnp.concatenate([prompt_kv, answer_kv[0], answer_kv[1]], axis=0)
    own_kinds, own_places = row_labels(
        block_index * block_rows, block_rows, prompt_rows, answer_rows
    )
    valid = (own_places < live_bound(own_kinds, lengths)).astype(jnp.float32)
    masked_grad = (cotangent * valid[:, None]).astype(jnp.bfloat16)

    def weights_for(pieces, first_row, row_lse):
        key_kinds, key_places = row_labels(first_row, pieces.shape[0], prompt_rows, answer_rows)
        allowed = visible(own_kinds, own_places, key_kinds, key_places, lengths)
        scores = contract_last(queries, pieces[:, :head_dim]) * scaling
        return jnp.exp(jnp.where(allowed, scores, -1e30) - row_lse[:, None])

    pieces = lax.all_gather(key_values[:, :head_dim], "blk", axis=0, tiled=True)
    row_max = jnp.full((block_rows,), -1e30, jnp.float32)
    key_kinds, key_places = row_labels(jnp.int32(0), pieces.shape[0], prompt_rows, answer_rows)
    allowed = visible(own_kinds, own_places, key_kinds, key_places, lengths)
    hidden_scores = jnp.where(allowed, contract_last(queries, pieces) * scaling, -1e30)
    new_max = jnp.maximum(row_max, jnp.max(hidden_scores, axis=1))
    fresh = jnp.sum(jnp.where(allowed, jnp.exp(hidden_scores - new_max[:, None]), 0.0), axis=1)
    row_lse = new_max + jnp.log(fresh)
    pieces = lax.all_gather(key_values, "blk", axis=0, tiled=True)
    weights = weights_for(pieces, jnp.int32(0), row_lse)
    values_part = pieces[:, head_dim:]
    summed = jnp.dot(weights.astype(jnp.bfloat16), values_part, preferred_element_type=jnp.float32)
    weight_grad = contract_last(masked_grad, values_part)
    summed, deltas = (summed, jnp.sum(weights * weight_grad, axis=1))
    pieces = lax.all_gather(key_values, "blk", axis=0, tiled=True)
    weights = weights_for(pieces, jnp.int32(0), row_lse)
    weight_grad = contract_last(masked_grad, pieces[:, head_dim:])
    score_grad = (weights * (weight_grad - deltas[:, None])).astype(jnp.bfloat16)
    query_sum = jnp.dot(score_grad, pieces[:, :head_dim], preferred_element_type=jnp.float32)
    own_keys = key_values[:, :head_dim]
    own_values = key_values[:, head_dim:]
    all_lse, all_deltas = (
        lax.all_gather(row_lse, "blk", axis=0, tiled=True),
        lax.all_gather(deltas, "blk", axis=0, tiled=True),
    )
    query_block = lax.all_gather(queries, "blk", axis=0, tiled=True)
    grad_block = lax.all_gather(masked_grad, "blk", axis=0, tiled=True)
    count = query_block.shape[0]
    query_kinds, query_places = row_labels(jnp.int32(0), count, prompt_rows, answer_rows)
    allowed = visible(query_kinds, query_places, own_kinds, own_places, lengths)
    scores = contract_last(query_block, own_keys) * scaling
    weights = jnp.exp(jnp.where(allowed, scores, -1e30) - all_lse[:, None])
    weight_grad = contract_last(grad_block, own_values)
    score_grad = (weights * (weight_grad - all_deltas[:, None])).astype(jnp.bfloat16)
    key_sum = contract_first(score_grad, query_block)
    value_sum = contract_first(weights.astype(jnp.bfloat16), grad_block)
    key_sum, value_sum = (key_sum, value_sum)
    key_sum, value_sum = lax.psum((key_sum, value_sum), "resp")
    output_rows = (summed * valid[:, None]).astype(jnp.bfloat16)
    query_grad_rows = (query_sum * scaling).astype(jnp.bfloat16)
    kv_grad = jnp.concatenate([key_sum * scaling, value_sum], axis=1).astype(jnp.bfloat16)
    middle = prompt_rows + answer_rows
    prompt_out = output_rows[:prompt_rows]
    answer_out = jnp.stack([output_rows[prompt_rows:middle], output_rows[middle:]])
    prompt_query_grad = query_grad_rows[:prompt_rows]
    answer_query_grad = jnp.stack([query_grad_rows[prompt_rows:middle], query_grad_rows[middle:]])
    prompt_kv_grad = kv_grad[:prompt_rows]
    answer_kv_grad = jnp.stack([kv_grad[prompt_rows:middle], kv_grad[middle:]])
    return (
        prompt_out,
        answer_out,
        prompt_query_grad,
        answer_query_grad,
        prompt_kv_grad,
        answer_kv_grad,
    )


def solution(mesh):
    in_specs = (
        P(("batch", "blk"), "resp"),
        P("batch", "blk", "resp"),
        P(("batch", "blk"), None),
        P("batch", "blk", None),
        P(("batch", "blk"), "resp"),
        P("batch", "blk", "resp"),
        P("batch"),
    )
    out_specs = (
        P(("batch", "blk"), "resp"),
        P("batch", "blk", "resp"),
        P(("batch", "blk"), "resp"),
        P("batch", "blk", "resp"),
        P(("batch", "blk"), None),
        P("batch", "blk", None),
    )
    return jax.shard_map(body, mesh=mesh, in_specs=in_specs, out_specs=out_specs, check_vma=False)
```

profile of v0, /device:TPU:1, one launch (start us, length us, event | category | flops | bytes accessed | tf_op | source)
XLA Modules:
  0.0 603.0 jit_solution(1901688313989410807)
XLA Ops:
  7.2 0.0 all-gather.7.cloned.1.call-start
  7.2 0.8 slice_bitcast_fusion.1
  8.0 0.8 pad_maximum_fusion
  8.8 0.0 copy-start.2
  8.8 0.7 slice.105
  9.5 0.0 all-gather.7.cloned.1.call-update
  9.5 0.0 all-gather.5.cloned.1.call-start
  9.6 0.0 copy-done.2
  9.6 0.7 all-gather.5.cloned.1.call-update
  10.3 0.0 all-gather.9.cloned.1.call-start
  10.3 0.7 slice_bitcast_fusion.9
  11.1 1.4 pad_maximum_fusion.2
  12.4 0.0 all-gather.9.cloned.1.call-update
  12.4 0.0 all-gather.11.cloned.1.call-start
  12.5 1.4 fusion.63
  13.8 2.0 fusion.61
  15.8 0.7 slice_bitcast_fusion.7
  16.6 1.5 multiply_convert_fusion.7
  18.0 0.0 all-gather.11.cloned.1.call-update
  18.0 0.0 all-reduce.5.cloned.1.call-start
  18.2 2.0 select_compare_fusion
  20.2 1.3 dynamic-slice
  22.1 105.6 %all-gather.7.cloned.1.call-done = bf16[7168,128]{1,0:T(8,128)(2,1)} async-done(((bf16[224,128]{1,0:T(8,128)(2,1)}), bf16[7168,128]{1,0:T(8,128)(2,1)}) %all-gather.7.cloned.1.call-update) | async-done | bytes 1835024 | tf_op jit(solution)/shard_map/all_gather | solution.py:70
  127.8 4.8 fusion.64
  132.6 0.0 copy-start.4
  132.6 4.2 select_reduce_fusion
  136.8 0.3 fusion.60
  137.1 0.0 copy-start.5
  137.1 126.0 %all-gather.5.cloned.1.call-done = bf16[7168,256]{1,0:T(8,128)(2,1)} async-done(((bf16[224,256]{1,0:T(8,128)(2,1)}), bf16[7168,256]{1,0:T(8,128)(2,1)}) %all-gather.5.cloned.1.call-update) | async-done | bytes 3670032 | tf_op jit(solution)/shard_map/all_gather | solution.py:78
  263.1 0.0 copy-done.4
  263.1 0.0 copy-start
  263.1 2.6 fusion.22
  265.7 0.0 copy-done.5
  265.7 0.0 copy-done
  265.7 4.2 multiply_reduce_fusion
  270.0 1.0 fusion.38
  271.0 0.6 slice.107
  271.6 0.0 copy-start.3
  271.6 1.1 fusion.35
  272.7 0.6 slice.110
  273.4 0.2 dynamic-update-slice.1
  273.5 95.5 %all-reduce.2 = (f32[7168]{0:T(1024)S(1)}, f32[7168]{0:T(1024)S(1)}) all-reduce(f32[7168]{0:T(1024)S(1)} %get-tuple-element.8, f32[7168]{0:T(1024)S(1)} %dynamic-update-slice.1), channel_id=1, replica_groups=mesh['blk'=32,'resp'=4,'batch'=4] {'blk'}, use_global_device_ids=true, to_apply=%add | all-reduce | flops 14336 | bytes 114688
  369.0 18.8 %all-gather.9.cloned.1.call-done = bf16[7168,128]{1,0:T(8,128)(2,1)} async-done(((bf16[224,128]{1,0:T(8,128)(2,1)}), bf16[7168,128]{1,0:T(8,128)(2,1)}) %all-gather.9.cloned.1.call-update) | async-done | bytes 1835024 | tf_op jit(solution)/shard_map/all_gather | solution.py:95
  387.9 0.0 copy-done.3
  387.9 7.2 %fusion.7 = f32[7168,224]{0,1:T(8,128)} fusion(bf16[7168,128]{1,0:T(8,128)(2,1)} %all-gather.9.cloned.1.call-done, f32[7168]{0:T(1024)S(1)} %get-tuple-element.6, s32[7168]{0:T(1024)S(1)} %get-tuple-element.36, s32[7168]{0:T(1024)S(1)} %get-tuple-element.35, s32[224]{0:T(256)S(1)} %get-tuple-element.31, s32[224]{0:T(256)S(1)} %get-tuple-element.32, ...), kind=kOutput, calls=%fused_computation.11 | convolution fusion | flops 428703744 | bytes 8411136 | tf_op jit(solution)/shard_map/dot_general | solution.py:37
  395.1 122.4 %all-gather.11.cloned.1.call-done = bf16[7168,128]{1,0:T(8,128)(2,1)} async-done(((bf16[224,128]{1,0:T(8,128)(2,1)}), bf16[7168,128]{1,0:T(8,128)(2,1)}) %all-gather.11.cloned.1.call-update) | async-done | bytes 1835024 | tf_op jit(solution)/shard_map/all_gather | solution.py:96
  517.5 0.0 copy-start.1
  517.5 6.5 %fusion.21 = f32[224,128]{1,0:T(8,128)} fusion(bf16[7168,128]{1,0:T(8,128)(2,1)} %all-gather.9.cloned.1.call-done, f32[7168,224]{0,1:T(8,128)} %fusion.7, bf16[7168,128]{1,0:T(8,128)(2,1)} %all-gather.11.cloned.1.call-done, f32[7168]{0:T(1024)S(1)} %get-tuple-element.7, bf16[224,256]{1,0:T(8,128)(2,1)S(1)} %copy-done.3), kind=kOutput, calls=%fused_computation.32 | convolution fusion | flops 826900480 | bytes 10293248 | tf_op jit(solution)/shard_map/dot_general | solution.py:43
  524.0 0.0 all-reduce.5.cloned.1.call-update
  524.0 0.6 pad_maximum_fusion.4
  524.6 0.6 pad_maximum_fusion.5
  525.3 0.0 copy-done.1
  525.3 3.8 fusion.16
  529.1 35.2 %psum.15 = bf16[224,128]{1,0:T(8,128)(2,1)S(1)} all-reduce(f32[224,128]{1,0:T(8,128)S(1)} %fusion.16), channel_id=1, replica_groups=mesh['blk'=32,'resp'=4,'batch'=4] {'resp'}, use_global_device_ids=true, to_apply=%region_4.5 | all-reduce | flops 28672 | bytes 172032 | tf_op jit(solution)/shard_map/psum | solution.py:107
  564.3 30.0 %all-reduce.5.cloned.1.call-done = f32[224,128]{1,0:T(8,128)} async-done(((f32[224,128]{1,0:T(8,128)}), f32[224,128]{1,0:T(8,128)}) %all-reduce.5.cloned.1.call-update) | async-done | bytes 114704 | tf_op jit(solution)/shard_map/psum | solution.py:107
  594.3 0.9 multiply_convert_fusion.6
  595.2 0.6 fusion.45
  595.9 0.6 pad_maximum_fusion.1
  (11 shorter events, 0.2 us)
Async XLA Ops:
  7.2 120.6 %all-gather.7.cloned.1.call-start = ((), (), s32[]{:S(2)}) async-start(), calls=%async_computation.1 | async-start | bytes 1892352 | tf_op jit(solution)/shard_map/all_gather | solution.py:70
  8.8 0.8 copy-start.2
  9.5 253.6 %all-gather.5.cloned.1.call-start = ((), (), s32[]{:S(2)}) async-start(), calls=%async_computation | async-start | bytes 3784704 | tf_op jit(solution)/shard_map/all_gather | solution.py:78
  10.3 377.6 %all-gather.9.cloned.1.call-start = ((), (), s32[]{:S(2)}) async-start(), calls=%async_computation.2 | async-start | bytes 1892352 | tf_op jit(solution)/shard_map/all_gather | solution.py:95
  12.4 505.1 %all-gather.11.cloned.1.call-start = ((), (), s32[]{:S(2)}) async-start(), calls=%async_computation.3 | async-start | bytes 1892352 | tf_op jit(solution)/shard_map/all_gather | solution.py:96
  18.0 576.3 %all-reduce.5.cloned.1.call-start = ((), (), s32[]{:S(2)}) async-start(), calls=%async_computation.4 | async-start | bytes 229376 | tf_op jit(solution)/shard_map/psum | solution.py:107
  132.6 130.5 %copy-start.4 = (bf16[224,128]{1,0:T(8,128)(2,1)S(1)}, bf16[224,128]{1,0:T(8,128)(2,1)}, u32[]{:S(2)}) copy-start(bf16[224,128]{1,0:T(8,128)(2,1)} %multiply_convert_fusion.7) | copy-start | bytes 172036
  137.1 128.7 %copy-start.5 = (bf16[96,128]{1,0:T(8,128)(2,1)S(1)}, bf16[96,128]{1,0:T(8,128)(2,1)}, u32[]{:S(2)}) copy-start(bf16[96,128]{1,0:T(8,128)(2,1)} %param.7) | copy-start | bytes 73732
  263.1 2.7 copy-start
  271.6 116.3 %copy-start.3 = (bf16[224,256]{1,0:T(8,128)(2,1)S(1)}, bf16[224,256]{1,0:T(8,128)(2,1)}, u32[]{:S(2)}) copy-start(bf16[224,256]{1,0:T(8,128)(2,1)} %copy-done.2) | copy-start | bytes 344068
  517.5 7.7 %copy-start.1 = (bf16[7168,128]{1,0:T(8,128)(2,1)S(1)}, bf16[7168,128]{1,0:T(8,128)(2,1)}, u32[]{:S(2)}) copy-start(bf16[7168,128]{1,0:T(8,128)(2,1)} %all-gather.11.cloned.1.call-done) | copy-start | bytes 5505028
Sparse Core Ops, SparseCore 0:
  10.1 117.6 all-gather.6
  129.8 133.1 all-gather.4
  265.2 122.6 all-gather.8
  390.4 127.0 all-gather.10
  524.1 70.1 all-reduce.4
where the time goes:
time: 604 us; the launch traced here: 603 us
  waiting for transfers between devices  404 us (67%)
  blocking collectives  131 us (22%)
  matrix products  31.3 us (5%)
  other arithmetic  15.5 us (3%)
  between operations  14.6 us (2%)
  local copies, waits for them, and re-layouts  7.01 us (1%)
    all_gather x1, waiting for transfers between devices, body(): pieces = lax.all_gather(key_values, 'blk', axis=0, tiled=True)  126 us
    all_gather x1, waiting for transfers between devices, body(): grad_block = lax.all_gather(masked_grad, 'blk', axis=0, tiled=True)  122 us
    all_gather x1, waiting for transfers between devices, body(): pieces = lax.all_gather(key_values[:, :head_dim], 'blk', axis=0, tiled=True)  106 us
    unnamed x1, blocking collectives  95.5 us
    psum x1, blocking collectives, body(): key_sum, value_sum = lax.psum((key_sum, value_sum), 'resp')  35.2 us
    psum x1, waiting for transfers between devices, body(): key_sum, value_sum = lax.psum((key_sum, value_sum), 'resp')  30 us
    dot_general x4, matrix products, contract_last(): lax.dot_general(left, right, (((1,), (1,)), ((), ())), preferred_element_...  18.9 us
    all_gather x1, waiting for transfers between devices, body(): query_block = lax.all_gather(queries, 'blk', axis=0, tiled=True)  18.8 us
  transfers between devices with their start and end apart: 5, of which 5 were waited for; matrix products, arithmetic and copies ran while one was open for 7% of the time, Pallas kernels for 0%

commit v1 on v0

v1 whole, which is shorter than its diff:
```python
import math

import jax
import jax.numpy as jnp
from jax import lax
from jax.experimental import pallas as pl
from jax.experimental.pallas import tpu as pltpu
from jax.sharding import PartitionSpec as P

MESH = pl.DeviceIdType.MESH
F32 = jnp.float32
BF16 = jnp.bfloat16
HIDDEN = -1e30
FLOOR = -1e20
RING = 16
PR, AR = 48, 32
BLOCK = PR + 2 * AR
QP, QA = 96, 64
OWN = QP + 2 * QA
ROWS = 4 * OWN
NP, NA = 4 * QP, 4 * QA
GROUPS, WIDTH = 4, 4

GATHER = {1: 0, 3: 0, 2: 3, 4: 3, 6: 3, 5: 6, 7: 6, 8: 6}
REDUCE = {1: 0, 3: 0, 6: 0, 2: 3, 4: 3, 5: 6, 7: 6, 8: 6}
ORDER = [1, 3, 2, 4, 6, 5, 7]
READY = [[1, 3], [2, 4], [6, 5], [7, 8]]
DONE = [[7, 8], [5, 6], [2, 4], [3, 1]]


def children(tree, parent):
    return sorted([o for o, p in tree.items() if p == parent], reverse=True)


SIGNED = [0] * 16
for _i, _o in enumerate(ORDER):
    SIGNED[1 + 2 * _i], SIGNED[2 + 2 * _i] = -_o, _o
SIGNED[15] = 8


def slot_of(offset, core):
    if offset == 8:
        return 15
    return 1 + 2 * ORDER.index(offset) + core


def dot_last(a, b):
    return lax.dot_general(a, b, (((1,), (1,)), ((), ())), preferred_element_type=F32)


def dot_first(a, b):
    return lax.dot_general(a, b, (((0,), (0,)), ((), ())), preferred_element_type=F32)


def dot(a, b):
    return jnp.dot(a, b, preferred_element_type=F32)


def kernel(
    pq, aq, pkv, akv, pg, ag, lens,
    po, ao, pqg, aqg, pkvg, akvg,
    kv, qg, q_all, g_all, pp, dpp, pa, dpa, stat, ot, st, dqt, own_f, osend, orecv,
    part, sib_out, sib_in, rs_out, rs_in, fin,
    loc, kv_r, kv_s, kv_x, qg_r, qg_s, st_r, st_s, o_r, o_s, sib_r, sib_s, rs_r, rs_s, fin_r, fin_s,
):
    blk, resp = lax.axis_index("blk"), lax.axis_index("resp")
    lo, z = blk // RING, lax.rem(blk, RING)
    hi, c = resp // 2, lax.rem(resp, 2)
    x = hi * 2 + lo
    s = 1 - 2 * c
    scaling = 1.0 / math.sqrt(128)

    def ring(step):
        return {"blk": lo * RING + lax.rem(z + step + 2 * RING, RING), "resp": resp}

    def across(step, core):
        to = lax.rem(x + step + 4, 4)
        return {"blk": lax.rem(to, 2) * RING + z, "resp": (to // 2) * 2 + core}

    sibling = {"blk": blk, "resp": hi * 2 + 1 - c}

    def remote(src, dst, send, recv, to):
        return pltpu.make_async_remote_copy(
            src_ref=src, dst_ref=dst, send_sem=send, recv_sem=recv, device_id=to, device_id_type=MESH
        )

    def guard(offset, act):
        if offset == 8:
            pl.when(c == 0)(act)
        else:
            act()

    first_p = pl.multiple_of(hi * PR, PR)
    first_a = pl.multiple_of(hi * AR, AR)
    pairs = [
        (pkv.at[pl.ds(first_p, PR)], kv.at[0, pl.ds(0, PR)]),
        (akv.at[0, pl.ds(first_a, AR)], kv.at[0, pl.ds(PR, AR)]),
        (akv.at[1, pl.ds(first_a, AR)], kv.at[0, pl.ds(PR + AR, AR)]),
    ]
    for j, (p_ref, a_ref) in enumerate(((pq, aq), (pg, ag))):
        cols = pl.ds(128 * j, 128)
        pairs.append((p_ref, qg.at[x, pl.ds(0, QP), cols]))
        pairs.append((a_ref.at[0], qg.at[x, pl.ds(QP, QA), cols]))
        pairs.append((a_ref.at[1], qg.at[x, pl.ds(QP + QA, QA), cols]))
    loads = [pltpu.make_async_copy(a, b, loc.at[i]) for i, (a, b) in enumerate(pairs)]
    for load in loads:
        load.start()

    barrier = pltpu.get_barrier_semaphore()
    steps = sorted({o - p for o, p in GATHER.items()})
    senders = [ring(-s * d) for d in steps] + [across(d, c) for d in (1, 2, 3)] + [sibling]
    for device in senders:
        pl.semaphore_signal(barrier, inc=1, device_id=device, device_id_type=MESH)
    for load in loads:
        load.wait()
    pl.semaphore_wait(barrier, len(senders))

    def hop(o):
        p = GATHER[o]
        src = kv.at[0] if p == 0 else kv.at[slot_of(p, c)]
        mine = slot_of(o, c)
        return remote(src, kv.at[mine], kv_s.at[o], kv_r.at[mine], ring(s * (o - p)))

    def share(o):
        mine = slot_of(o, c)
        return remote(kv.at[mine], kv.at[mine], kv_x.at[o], kv_r.at[mine], sibling)

    def theirs(o):
        other = slot_of(o, 1 - c)
        pltpu.make_async_copy(kv.at[other], kv.at[other], kv_r.at[other]).wait()

    def arrive(o):
        def act():
            hop(o).wait_recv()
            for o2 in children(GATHER, o):
                guard(o2, lambda o2=o2: hop(o2).start())
            share(o).start()

        guard(o, act)

    def arrived(o):
        if o == 8:
            pl.when(c == 1)(lambda: theirs(8))
        else:
            theirs(o)

    for o in children(GATHER, 0):
        guard(o, lambda o=o: hop(o).start())
    sends_q = [
        remote(qg.at[x], qg.at[x], qg_s.at[d], qg_r.at[d], across(d, c)) for d in (1, 2, 3)
    ]
    for d in (1, 0, 2):
        sends_q[d].start()

    for o in READY[0]:
        arrive(o)
    for copy in sends_q:
        copy.wait_recv()

    for d in range(4):
        place = ((d % 2) * RING + z) * QA + lax.broadcasted_iota(jnp.int32, (QA, 128), 0)
        q_all[pl.ds(d * QP, QP)] = qg[d, pl.ds(0, QP), pl.ds(0, 128)]
        g_all[pl.ds(d * QP, QP)] = qg[d, pl.ds(0, QP), pl.ds(128, 128)]
        for k in range(2):
            rows = pl.ds(NP + k * NA + d * QA, QA)
            q_all[rows] = qg[d, pl.ds(QP + k * QA, QA), pl.ds(0, 128)]
            masked = jnp.where(
                place < lens[k + 1], qg[d, pl.ds(QP + k * QA, QA), pl.ds(128, 128)].astype(F32), 0.0
            )
            g_all[rows] = masked.astype(BF16)

    lane = lax.broadcasted_iota(jnp.int32, (1, NP), 1)
    which = (lane >= QP).astype(jnp.int32) + (lane >= 2 * QP) + (lane >= 3 * QP)
    q_place_p = (which & 1) * (RING * QP) + z * QP + lane - which * QP
    lane = lax.broadcasted_iota(jnp.int32, (1, NA), 1)
    which = (lane >= QA).astype(jnp.int32) + (lane >= 2 * QA) + (lane >= 3 * QA)
    q_place_a = (which & 1) * (RING * QA) + z * QA + lane - which * QA

    def key_ring(slot):
        off = jnp.int32(0)
        for k in range(1, 16):
            off = jnp.where(slot == k, SIGNED[k], off)
        return lo * RING + lax.rem(z + off + RING, RING)

    def kind_rows(ref, base, k):
        start, count = (0, PR) if k == 0 else (PR + (k - 1) * AR, AR)
        block = ref[pl.ds(base, WIDTH), pl.ds(start, count), :]
        return block.reshape(WIDTH * count, 256)

    iota_p = lax.broadcasted_iota(jnp.int32, (PR, NP), 0)
    iota_a = lax.broadcasted_iota(jnp.int32, (AR, NA), 0)

    def forward(g, _):
        for k in range(GROUPS):

            @pl.when(g == k)
            def _(k=k):
                if k:
                    for o in READY[k]:
                        arrive(o)
                for o in READY[k]:
                    arrived(o)

        base = g * WIDTH
        blocks = [key_ring(base + j) for j in range(WIDTH)]
        rows_p = kind_rows(kv, base, 0)
        keys, values = rows_p[:, :128], rows_p[:, 128:]
        sp = dot_last(keys, q_all[...]) * scaling
        causal = jnp.concatenate(
            [
                jnp.where(
                    iota_p <= q_place_p - (blocks[j] * QP + hi * PR),
                    sp[j * PR : (j + 1) * PR, :NP],
                    HIDDEN,
                )
                for j in range(WIDTH)
            ],
            axis=0,
        )
        sp = jnp.concatenate([causal, sp[:, NP:]], axis=1)
        top = jnp.max(sp, axis=0, keepdims=True)
        sa, kinds = [], []
        for k in range(2):
            rows_a = kind_rows(kv, base, k + 1)
            kinds.append(rows_a)
            sk = dot_last(rows_a[:, :128], q_all[pl.ds(NP + k * NA, NA)]) * scaling
            pieces = []
            for j in range(WIDTH):
                start = blocks[j] * QA + hi * AR
                bound = jnp.minimum(q_place_a, lens[k + 1] - 1) - start
                pieces.append(jnp.where(iota_a <= bound, sk[j * AR : (j + 1) * AR], HIDDEN))
            sa.append(jnp.concatenate(pieces, axis=0))
        tops = [top[:, :NP]]
        for k in range(2):
            a, b = NP + k * NA, NP + (k + 1) * NA
            tops.append(jnp.maximum(top[:, a:b], jnp.max(sa[k], axis=0, keepdims=True)))
        top = jnp.maximum(jnp.concatenate(tops, axis=1), FLOOR)
        wp = jnp.exp(sp - top)
        dp = dot_last(values, g_all[...])
        pp[g] = wp
        dpp[g] = dp
        total = jnp.sum(wp, axis=0, keepdims=True)
        delta = jnp.sum(wp * dp, axis=0, keepdims=True)
        out = dot_first(values, wp.astype(BF16))
        totals, deltas, outs = [total[:, :NP]], [delta[:, :NP]], [out[:, :NP]]
        for k in range(2):
            a, b = NP + k * NA, NP + (k + 1) * NA
            wa = jnp.exp(sa[k] - top[:, a:b])
            da = dot_last(kinds[k][:, 128:], g_all[pl.ds(a, NA)])
            pa[g, k] = wa
            dpa[g, k] = da
            totals.append(total[:, a:b] + jnp.sum(wa, axis=0, keepdims=True))
            deltas.append(delta[:, a:b] + jnp.sum(wa * da, axis=0, keepdims=True))
            outs.append(out[:, a:b] + dot_first(kinds[k][:, 128:], wa.astype(BF16)))
        stat[g, pl.ds(0, 1)] = top
        stat[g, pl.ds(1, 1)] = jnp.concatenate(totals, axis=1)
        stat[g, pl.ds(2, 1)] = jnp.concatenate(deltas, axis=1)
        ot[g] = jnp.concatenate(outs, axis=1)
        return 0

    lax.fori_loop(0, GROUPS, forward, 0)

    def merge(ref, count):
        top = ref[0, pl.ds(0, 1)]
        for i in range(1, count):
            top = jnp.maximum(top, ref[i, pl.ds(0, 1)])
        factors = [jnp.exp(ref[i, pl.ds(0, 1)] - top) for i in range(count)]
        total = sum(f * ref[i, pl.ds(1, 1)] for i, f in enumerate(factors))
        delta = sum(f * ref[i, pl.ds(2, 1)] for i, f in enumerate(factors))
        return top, total, delta, factors

    top, total, delta, factors = merge(stat, GROUPS)
    st[0, pl.ds(0, 1)] = top
    st[0, pl.ds(1, 1)] = total
    st[0, pl.ds(2, 1)] = delta
    sends_st = [
        remote(st.at[0], st.at[d], st_s.at[d], st_r.at[d], across(d, c)) for d in (1, 2, 3)
    ]
    for d in (1, 0, 2):
        sends_st[d].start()
    ot[0] = sum(f * ot[i] for i, f in enumerate(factors))
    dqt[...] = jnp.zeros_like(dqt)
    for copy in sends_st:
        copy.wait_recv()
    all_top, total, delta, _ = merge(st, 4)
    delta = delta / total
    scale_own = jnp.exp(top - all_top) / total
    for i in range(GROUPS):
        stat[i, pl.ds(3, 1)] = jnp.exp(stat[i, pl.ds(0, 1)] - all_top) / total

    def pass_on(o):
        mine = slot_of(o, c)
        return remote(sib_out.at[o], sib_in.at[o], sib_s.at[o], sib_r.at[o], sibling)

    def offer(o):
        def act():
            sib_out[o] = part[slot_of(o, 1 - c)].astype(BF16)
            pass_on(o).start()

        if o == 8:
            pl.when(c == 1)(act)
        else:
            act()

    def up(o):
        return remote(
            rs_out.at[o], rs_in.at[o], rs_s.at[o], rs_r.at[o], ring(-s * (o - REDUCE[o]))
        )

    def send_up(o):
        def act():
            pass_on(o).wait_recv()
            value = part[slot_of(o, c)] + sib_in[o].astype(F32)
            if o < 8:
                for o2 in children(REDUCE, o):
                    if o2 < 8:
                        up(o2).wait_recv()
                        value = value + rs_in[o2].astype(F32)
            part[slot_of(o, c)] = value
            if 8 in children(REDUCE, o):

                @pl.when(c == 0)
                def _():
                    up(8).wait_recv()
                    part[slot_of(o, c)] = part[slot_of(o, c)] + rs_in[8].astype(F32)

            rs_out[o] = part[slot_of(o, c)].astype(BF16)
            up(o).start()

        guard(o, act)

    def backward(i, _):
        g = GROUPS - 1 - i
        base = g * WIDTH
        rows_p = kind_rows(kv, base, 0)
        keys = rows_p[:, :128]
        factor = stat[g, pl.ds(3, 1)]
        w = pp[g] * factor
        ds = (w * (dpp[g] - delta)).astype(BF16)
        part[pl.ds(base, WIDTH), pl.ds(0, PR), pl.ds(0, 128)] = dot(ds, q_all[...]).reshape(
            WIDTH, PR, 128
        )
        part[pl.ds(base, WIDTH), pl.ds(0, PR), pl.ds(128, 128)] = dot(
            w.astype(BF16), g_all[...]
        ).reshape(WIDTH, PR, 128)
        dq = dot_first(keys, ds)
        dqs = [dq[:, :NP]]
        for k in range(2):
            a, b = NP + k * NA, NP + (k + 1) * NA
            rows_a = kind_rows(kv, base, k + 1)
            w = pa[g, k] * factor[:, a:b]
            ds = (w * (dpa[g, k] - delta[:, a:b])).astype(BF16)
            where = pl.ds(PR + k * AR, AR)
            part[pl.ds(base, WIDTH), where, pl.ds(0, 128)] = dot(
                ds, q_all[pl.ds(a, NA)]
            ).reshape(WIDTH, AR, 128)
            part[pl.ds(base, WIDTH), where, pl.ds(128, 128)] = dot(
                w.astype(BF16), g_all[pl.ds(a, NA)]
            ).reshape(WIDTH, AR, 128)
            dqs.append(dq[:, a:b] + dot_first(rows_a[:, :128], ds))
        dqt[...] += jnp.concatenate(dqs, axis=1)
        for k in range(GROUPS):

            @pl.when(i == k)
            def _(k=k):
                for o in DONE[k]:
                    offer(o)
                if k:
                    for o in DONE[k - 1]:
                        if not children(REDUCE, o):
                            send_up(o)

        return 0

    lax.fori_loop(0, GROUPS, backward, 0)
    for o in DONE[GROUPS - 1]:
        if not children(REDUCE, o):
            send_up(o)

    backs = []
    for j, whole in enumerate((ot[0] * scale_own, dqt[...])):
        rows = whole.T
        for d in range(4):
            for start, count, at in (
                (d * QP, QP, 0),
                (NP + d * QA, QA, QP),
                (NP + NA + d * QA, QA, QP + QA),
            ):
                piece = rows[start : start + count]
                own_f[j, d, pl.ds(at, count)] = piece
                osend[j, d, pl.ds(at, count)] = piece.astype(BF16)
        for d in (2, 1, 3):
            theirs_x = lax.rem(x + 4 - d, 4)
            back = remote(
                osend.at[j, theirs_x], orecv.at[j, d], o_s.at[j, d], o_r.at[j, d], across(-d, c)
            )
            back.start()
            backs.append(back)

    for o in sorted(REDUCE, reverse=True):
        if children(REDUCE, o):
            send_up(o)

    for back in backs:
        back.wait_recv()
    place = blk * QA + lax.broadcasted_iota(jnp.int32, (QA, 128), 0)
    for j, (p_out, a_out) in enumerate(((po, ao), (pqg, aqg))):
        value = own_f[j, x]
        for d in (1, 2, 3):
            value = value + orecv[j, d].astype(F32)
        if j:
            value = value * scaling
        p_out[...] = value[:QP].astype(BF16)
        for k in range(2):
            rows = value[QP + k * QA : QP + (k + 1) * QA]
            if j == 0:
                rows = jnp.where(place < lens[k + 1], rows, 0.0)
            a_out[k] = rows.astype(BF16)

    value = part[0]
    for o in children(REDUCE, 0)[::-1]:
        up(o).wait_recv()
        value = value + rs_in[o].astype(F32)
    fin[0, c] = value.astype(BF16)
    finals = [
        remote(fin.at[0, c], fin.at[0, c], fin_s.at[0], fin_r.at[0], sibling),
        remote(fin.at[0, c], fin.at[1, c], fin_s.at[1], fin_r.at[1], across(2, c)),
        remote(fin.at[0, c], fin.at[1, c], fin_s.at[2], fin_r.at[2], across(2, 1 - c)),
    ]
    for f in finals[::-1]:
        f.start()
    for f in finals:
        f.wait_recv()
    factor = jnp.where(lax.broadcasted_iota(jnp.int32, (1, 256), 1) < 128, scaling, 1.0)
    for h in range(2):
        half = hi if h == 0 else 1 - hi
        value = ((fin[h, 0].astype(F32) + fin[h, 1].astype(F32)) * factor).astype(BF16)
        pkvg[pl.ds(pl.multiple_of(half * PR, PR), PR)] = value[:PR]
        for k in range(2):
            akvg[k, pl.ds(pl.multiple_of(half * AR, AR), AR)] = value[
                PR + k * AR : PR + (k + 1) * AR
            ]

    for copy in sends_q + sends_st + backs + finals:
        copy.wait_send()
    for o in GATHER:
        def act(o=o):
            hop(o).wait_send()
            share(o).wait_send()
            up(o).wait_send()

        guard(o, act)
        if o == 8:
            pl.when(c == 1)(lambda: pass_on(8).wait_send())
        else:
            pass_on(o).wait_send()


def body(*args):
    vmem = pl.BlockSpec(memory_space=pltpu.VMEM)
    hbm = pl.BlockSpec(memory_space=pl.ANY)
    dma = pltpu.SemaphoreType.DMA
    outs = (
        jax.ShapeDtypeStruct((QP, 128), BF16),
        jax.ShapeDtypeStruct((2, QA, 128), BF16),
        jax.ShapeDtypeStruct((QP, 128), BF16),
        jax.ShapeDtypeStruct((2, QA, 128), BF16),
        jax.ShapeDtypeStruct((QP, 256), BF16),
        jax.ShapeDtypeStruct((2, QA, 256), BF16),
    )
    return pl.pallas_call(
        kernel,
        out_shape=outs,
        in_specs=[hbm] * 6 + [pl.BlockSpec(memory_space=pltpu.SMEM)],
        out_specs=(vmem,) * 6,
        scratch_shapes=[
            pltpu.VMEM((16, BLOCK, 256), BF16),
            pltpu.VMEM((4, OWN, 256), BF16),
            pltpu.VMEM((ROWS, 128), BF16),
            pltpu.VMEM((ROWS, 128), BF16),
            pltpu.VMEM((GROUPS, WIDTH * PR, ROWS), F32),
            pltpu.VMEM((GROUPS, WIDTH * PR, ROWS), F32),
            pltpu.VMEM((GROUPS, 2, WIDTH * AR, NA), F32),
            pltpu.VMEM((GROUPS, 2, WIDTH * AR, NA), F32),
            pltpu.VMEM((GROUPS, 8, ROWS), F32),
            pltpu.VMEM((GROUPS, 128, ROWS), F32),
            pltpu.VMEM((4, 8, ROWS), F32),
            pltpu.VMEM((128, ROWS), F32),
            pltpu.VMEM((2, 4, OWN, 128), F32),
            pltpu.VMEM((2, 4, OWN, 128), BF16),
            pltpu.VMEM((2, 4, OWN, 128), BF16),
            pltpu.VMEM((16, BLOCK, 256), F32),
            pltpu.VMEM((9, BLOCK, 256), BF16),
            pltpu.VMEM((9, BLOCK, 256), BF16),
            pltpu.VMEM((9, BLOCK, 256), BF16),
            pltpu.VMEM((9, BLOCK, 256), BF16),
            pltpu.VMEM((2, 2, BLOCK, 256), BF16),
            dma((9,)),
            dma((16,)),
            dma((9,)),
            dma((9,)),
            dma((4,)),
            dma((4,)),
            dma((4,)),
            dma((4,)),
            dma((2, 4)),
            dma((2, 4)),
            dma((9,)),
            dma((9,)),
            dma((9,)),
            dma((9,)),
            dma((3,)),
            dma((3,)),
        ],
        compiler_params=pltpu.CompilerParams(
            collective_id=0, has_side_effects=True, vmem_limit_bytes=56 * 2**20
        ),
    )(*args)


def solution(mesh):
    row = P(("batch", "blk"), "resp")
    answer = P("batch", "blk", "resp")
    row_kv = P(("batch", "blk"), None)
    answer_kv = P("batch", "blk", None)
    return jax.shard_map(
        body,
        mesh=mesh,
        in_specs=(row, answer, row_kv, answer_kv, row, answer, P("batch")),
        out_specs=(row, answer, row, answer, row_kv, answer_kv),
        check_vma=False,
    )
```

time: 604 us -> 63.9 us (0.11)
  waiting for transfers between devices: 404 us -> 0 us
  blocking collectives: 131 us -> 0 us
  Pallas kernels: 0 us -> 57.9 us
  matrix products: 31.3 us -> 0 us
  other arithmetic: 15.5 us -> 0 us
  between operations: 14.6 us -> 0.66 us
    all_gather x4 -> x0, waiting for transfers between devices: 373 us -> none  [the longest x1 126 us: body(): pieces = lax.all_gather(key_values, 'blk', axis=0, tiled=True)]
    unnamed x1 -> x0, blocking collectives: 95.5 us -> none
    pallas_call x0 -> x1, Pallas kernels: none -> 57.9 us  [body(): pl.pallas_call(kernel, out_shape=outs, in_specs=[hbm] * 6 + [pl.BlockSpec...]
    psum x1 -> x0, blocking collectives: 35.2 us -> none  [body(): key_sum, value_sum = lax.psum((key_sum, value_sum), 'resp')]
    dot_general x8 -> x0, matrix products: 31.3 us -> none  [the longest x4 18.9 us: contract_last(): lax.dot_general(left, right, (((1,), (1,)), ((), ())), preferred_element_...]
    psum x1 -> x0, waiting for transfers between devices: 30 us -> none  [body(): key_sum, value_sum = lax.psum((key_sum, value_sum), 'resp')]
  transfers between devices with their start and end apart: 5 -> 0, of which waited for: 5 -> 0; matrix products, arithmetic and copies ran while one was open for 7% -> 0% of each run, Pallas kernels for 0% -> 0%
where the time goes in v1:
time: 63.9 us; the launch traced here: 63.3 us
  Pallas kernels  57.9 us (91%)
  local copies, waits for them, and re-layouts  4.82 us (8%)
  between operations  0.66 us (1%)
    pallas_call x1, Pallas kernels, body(): pl.pallas_call(kernel, out_shape=outs, in_specs=[hbm] * 6 + [pl.BlockSpec...  57.9 us
    unnamed x16, local copies, waits for them, and re-layouts  4.82 us

profile of v1, /device:TPU:1, one launch (start us, length us, event | category | flops | bytes accessed | tf_op | source)
XLA Modules:
  0.0 63.3 jit_solution(173527401799733070)
XLA Ops:
  0.6 57.9 %shard_map.118 = (bf16[96,128]{1,0:T(8,128)(2,1)}, bf16[2,64,128]{2,1,0:T(8,128)(2,1)}, bf16[96,128]{1,0:T(8,128)(2,1)}, bf16[2,64,128]{2,1,0:T(8,128)(2,1)}, bf...) custom-call(bf16[96,128]{1,0:T(8,128)(2,1)} %pq.1, bf16[2,64,128]{2,1,0:T(8,128)(2,1)} %aq.1, bf16[96,256]{1,0:T(8,128)(2,1)} %pkv.1, ...), custom_call_target="tpu_custom_call" | custom-call | tf_op jit(solution)/shard_map/pallas_call | solution.py:471
  58.5 0.0 copy-start.3
  58.5 1.4 %copy.19 = bf16[96,128]{1,0:T(8,128)(2,1)} copy(bf16[96,128]{1,0:T(8,128)(2,1)} %get-tuple-element.12) | data formatting | bytes 49152
  59.9 0.0 copy-done.3
  59.9 0.0 copy-start.4
  59.9 0.0 copy-start.2
  59.9 0.6 copy.20
  60.5 0.1 copy-done.4
  60.6 0.0 copy-start.1
  60.6 0.6 copy.21
  61.2 0.0 copy-done.2
  61.2 0.6 copy.22
  61.9 0.0 copy-done.1
  61.9 0.0 copy-start
  61.9 0.6 copy.23
  62.5 0.2 copy-done
  62.7 0.6 copy.24
Async XLA Ops:
  58.5 1.4 %copy-start.3 = (bf16[2,64,128]{2,1,0:T(8,128)(2,1)S(1)}, bf16[2,64,128]{2,1,0:T(8,128)(2,1)}, u32[]{:S(2)}) copy-start(bf16[2,64,128]{2,1,0:T(8,128)(2,1)} %get-tuple-element.13) | copy-start | bytes 98308
  59.9 0.8 %copy-start.4 = (bf16[96,128]{1,0:T(8,128)(2,1)S(1)}, bf16[96,128]{1,0:T(8,128)(2,1)}, u32[]{:S(2)}) copy-start(bf16[96,128]{1,0:T(8,128)(2,1)} %get-tuple-element.14) | copy-start | bytes 73732
  59.9 1.4 %copy-start.2 = (bf16[2,64,128]{2,1,0:T(8,128)(2,1)S(1)}, bf16[2,64,128]{2,1,0:T(8,128)(2,1)}, u32[]{:S(2)}) copy-start(bf16[2,64,128]{2,1,0:T(8,128)(2,1)} %get-tuple-element.15) | copy-start | bytes 98308
  60.6 1.2 %copy-start.1 = (bf16[96,256]{1,0:T(8,128)(2,1)S(1)}, bf16[96,256]{1,0:T(8,128)(2,1)}, u32[]{:S(2)}) copy-start(bf16[96,256]{1,0:T(8,128)(2,1)} %get-tuple-element.16) | copy-start | bytes 147460
  61.9 0.9 %copy-start = (bf16[2,64,256]{2,1,0:T(8,128)(2,1)S(1)}, bf16[2,64,256]{2,1,0:T(8,128)(2,1)}, u32[]{:S(2)}) copy-start(bf16[2,64,256]{2,1,0:T(8,128)(2,1)} %get-tuple-element.17) | copy-start | bytes 196612

commit v2 on v1

--- a/solution.py
+++ b/solution.py
@@ -1,3 +1,4 @@
+import functools
 import math
 
 import jax
@@ -19,13 +20,14 @@
 OWN = QP + 2 * QA
 ROWS = 4 * OWN
 NP, NA = 4 * QP, 4 * QA
+PARCELS = ((0, PR), (PR, 2 * AR))
+PIECES = ((0, PR), (PR, 2 * AR))
+WINDOW = 2 * AR
 GROUPS, WIDTH = 4, 4
 
 GATHER = {1: 0, 3: 0, 2: 3, 4: 3, 6: 3, 5: 6, 7: 6, 8: 6}
 REDUCE = {1: 0, 3: 0, 6: 0, 2: 3, 4: 3, 5: 6, 7: 6, 8: 6}
 ORDER = [1, 3, 2, 4, 6, 5, 7]
-READY = [[1, 3], [2, 4], [6, 5], [7, 8]]
-DONE = [[7, 8], [5, 6], [2, 4], [3, 1]]
 
 
 def children(tree, parent):
@@ -44,6 +46,11 @@
     return 1 + 2 * ORDER.index(offset) + core
 
 
+READY = [[o for o in GATHER if min(slot_of(o, 0), 15) // WIDTH == k] for k in range(GROUPS)]
+DONE = READY[::-1]
+RELAYS = [o for o in ORDER if children(GATHER, o)]
+
+
 def dot_last(a, b):
     return lax.dot_general(a, b, (((1,), (1,)), ((), ())), preferred_element_type=F32)
 
@@ -60,8 +67,8 @@
     pq, aq, pkv, akv, pg, ag, lens,
     po, ao, pqg, aqg, pkvg, akvg,
     kv, qg, q_all, g_all, pp, dpp, pa, dpa, stat, ot, st, dqt, own_f, osend, orecv,
-    part, sib_out, sib_in, rs_out, rs_in, fin,
-    loc, kv_r, kv_s, kv_x, qg_r, qg_s, st_r, st_s, o_r, o_s, sib_r, sib_s, rs_r, rs_s, fin_r, fin_s,
+    part, sib_out, sib_in, rs_out, rs_in, fin, own_in,
+    loc, kv_r, kv_s, kv_x, qg_r, qg_s, st_r, st_s, o_r, o_s, sib_r, sib_s, rs_r, rs_s, fin_r, fin_s, own_r, own_s,
 ):
     blk, resp = lax.axis_index("blk"), lax.axis_index("resp")
     lo, z = blk // RING, lax.rem(blk, RING)
@@ -115,45 +122,48 @@
         load.wait()
     pl.semaphore_wait(barrier, len(senders))
 
-    def hop(o):
+    def rows_of(piece):
+        return pl.ds(*PIECES[piece])
+
+    def hop(o, piece):
         p = GATHER[o]
-        src = kv.at[0] if p == 0 else kv.at[slot_of(p, c)]
-        mine = slot_of(o, c)
-        return remote(src, kv.at[mine], kv_s.at[o], kv_r.at[mine], ring(s * (o - p)))
-
-    def share(o):
-        mine = slot_of(o, c)
-        return remote(kv.at[mine], kv.at[mine], kv_x.at[o], kv_r.at[mine], sibling)
+        source = 0 if p == 0 else slot_of(p, c)
+        mine, rows = slot_of(o, c), pl.ds(*PARCELS[piece])
+        return remote(
+            kv.at[source, rows], kv.at[mine, rows], kv_s.at[piece, o], kv_r.at[piece, mine], ring(s * (o - p))
+        )
+
+    def share(o, piece):
+        mine, rows = slot_of(o, c), pl.ds(*PARCELS[piece])
+        return remote(kv.at[mine, rows], kv.at[mine, rows], kv_x.at[piece, o], kv_r.at[piece, mine], sibling)
+
+    def arrive(o):
+        for piece in range(len(PARCELS)):
+            hop(o, piece).wait_recv()
+            for o2 in children(GATHER, o):
+                hop(o2, piece).start()
+            if o != 8:
+                share(o, piece).start()
 
     def theirs(o):
         other = slot_of(o, 1 - c)
-        pltpu.make_async_copy(kv.at[other], kv.at[other], kv_r.at[other]).wait()
-
-    def arrive(o):
-        def act():
-            hop(o).wait_recv()
-            for o2 in children(GATHER, o):
-                guard(o2, lambda o2=o2: hop(o2).start())
-            share(o).start()
-
-        guard(o, act)
-
-    def arrived(o):
-        if o == 8:
-            pl.when(c == 1)(lambda: theirs(8))
-        else:
-            theirs(o)
-
-    for o in children(GATHER, 0):
-        guard(o, lambda o=o: hop(o).start())
+        for piece in range(len(PARCELS)):
+            block = kv.at[other, pl.ds(*PARCELS[piece])]
+            pltpu.make_async_copy(block, block, kv_r.at[piece, other]).wait()
+
     sends_q = [
         remote(qg.at[x], qg.at[x], qg_s.at[d], qg_r.at[d], across(d, c)) for d in (1, 2, 3)
     ]
     for d in (1, 0, 2):
         sends_q[d].start()
-
+    for piece in range(len(PARCELS)):
+        for o in children(GATHER, 0):
+            hop(o, piece).start()
+    for o in RELAYS:
+        arrive(o)
     for o in READY[0]:
-        arrive(o)
+        if o not in RELAYS:
+            arrive(o)
     for copy in sends_q:
         copy.wait_recv()
 
@@ -190,17 +200,20 @@
     iota_p = lax.broadcasted_iota(jnp.int32, (PR, NP), 0)
     iota_a = lax.broadcasted_iota(jnp.int32, (AR, NA), 0)
 
-    def forward(g, _):
+    def receive(g):
         for k in range(GROUPS):
 
             @pl.when(g == k)
             def _(k=k):
                 if k:
                     for o in READY[k]:
-                        arrive(o)
+                        if o not in RELAYS:
+                            arrive(o)
                 for o in READY[k]:
-                    arrived(o)
-
+                    if o != 8:
+                        theirs(o)
+
+    def attend(g):
         base = g * WIDTH
         blocks = [key_ring(base + j) for j in range(WIDTH)]
         rows_p = kind_rows(kv, base, 0)
@@ -256,23 +269,27 @@
         stat[g, pl.ds(1, 1)] = jnp.concatenate(totals, axis=1)
         stat[g, pl.ds(2, 1)] = jnp.concatenate(deltas, axis=1)
         ot[g] = jnp.concatenate(outs, axis=1)
+
+    def forward(g, _):
+        receive(g)
+        attend(g)
         return 0
 
     lax.fori_loop(0, GROUPS, forward, 0)
 
-    def merge(ref, count):
-        top = ref[0, pl.ds(0, 1)]
-        for i in range(1, count):
-            top = jnp.maximum(top, ref[i, pl.ds(0, 1)])
-        factors = [jnp.exp(ref[i, pl.ds(0, 1)] - top) for i in range(count)]
-        total = sum(f * ref[i, pl.ds(1, 1)] for i, f in enumerate(factors))
-        delta = sum(f * ref[i, pl.ds(2, 1)] for i, f in enumerate(factors))
+    def merge(parts):
+        top = functools.reduce(jnp.maximum, [p[0] for p in parts])
+        factors = [jnp.exp(p[0] - top) for p in parts]
+        total = sum(f * p[1] for f, p in zip(factors, parts))
+        delta = sum(f * p[2] for f, p in zip(factors, parts))
         return top, total, delta, factors
 
-    top, total, delta, factors = merge(stat, GROUPS)
-    st[0, pl.ds(0, 1)] = top
-    st[0, pl.ds(1, 1)] = total
-    st[0, pl.ds(2, 1)] = delta
+    top, total, delta, factors = merge(
+        [[stat[i, pl.ds(k, 1)] for k in range(3)] for i in range(GROUPS)]
+    )
+    st[0, 0] = top
+    st[0, 1] = total
+    st[0, 2] = delta
     sends_st = [
         remote(st.at[0], st.at[d], st_s.at[d], st_r.at[d], across(d, c)) for d in (1, 2, 3)
     ]
@@ -282,7 +299,7 @@
     dqt[...] = jnp.zeros_like(dqt)
     for copy in sends_st:
         copy.wait_recv()
-    all_top, total, delta, _ = merge(st, 4)
+    all_top, total, delta, _ = merge([[st[d, k] for k in range(3)] for d in range(4)])
     delta = delta / total
     scale_own = jnp.exp(top - all_top) / total
     for i in range(GROUPS):
@@ -302,35 +319,44 @@
         else:
             act()
 
-    def up(o):
+    def up(o, piece, direction=None):
+        rows = rows_of(piece)
+        step = -s * (o - REDUCE[o])
+        if REDUCE[o] == 0:
+            to = {"blk": lo * RING + lax.rem(z + step + 2 * RING, RING), "resp": hi * 2 + piece}
+        else:
+            to = ring(step)
+        way = c if direction is None else direction
         return remote(
-            rs_out.at[o], rs_in.at[o], rs_s.at[o], rs_r.at[o], ring(-s * (o - REDUCE[o]))
+            rs_out.at[o, rows], rs_in.at[way, o, rows], rs_s.at[piece, o], rs_r.at[way, piece, o], to
         )
 
     def send_up(o):
         def act():
             pass_on(o).wait_recv()
-            value = part[slot_of(o, c)] + sib_in[o].astype(F32)
-            if o < 8:
+            mine = slot_of(o, c)
+            for piece in range(2):
+                rows = rows_of(piece)
+                value = part[mine, rows] + sib_in[o, rows].astype(F32)
                 for o2 in children(REDUCE, o):
                     if o2 < 8:
-                        up(o2).wait_recv()
-                        value = value + rs_in[o2].astype(F32)
-            part[slot_of(o, c)] = value
-            if 8 in children(REDUCE, o):
-
-                @pl.when(c == 0)
-                def _():
-                    up(8).wait_recv()
-                    part[slot_of(o, c)] = part[slot_of(o, c)] + rs_in[8].astype(F32)
-
-            rs_out[o] = part[slot_of(o, c)].astype(BF16)
-            up(o).start()
+                        up(o2, piece).wait_recv()
+                        value = value + rs_in[c, o2, rows].astype(F32)
+                if 8 in children(REDUCE, o):
+                    part[mine, rows] = value
+
+                    @pl.when(c == 0)
+                    def _(piece=piece, rows=rows):
+                        up(8, piece).wait_recv()
+                        part[mine, rows] = part[mine, rows] + rs_in[0, 8, rows].astype(F32)
+
+                    value = part[mine, rows]
+                rs_out[o, rows] = value.astype(BF16)
+                up(o, piece).start()
 
         guard(o, act)
 
-    def backward(i, _):
-        g = GROUPS - 1 - i
+    def differentiate(g):
         base = g * WIDTH
         rows_p = kind_rows(kv, base, 0)
         keys = rows_p[:, :128]
@@ -359,6 +385,8 @@
             ).reshape(WIDTH, AR, 128)
             dqs.append(dq[:, a:b] + dot_first(rows_a[:, :128], ds))
         dqt[...] += jnp.concatenate(dqs, axis=1)
+
+    def reduce(i):
         for k in range(GROUPS):
 
             @pl.when(i == k)
@@ -370,9 +398,15 @@
                         if not children(REDUCE, o):
                             send_up(o)
 
+    def backward(i, _):
+        differentiate(GROUPS - 1 - i)
+        reduce(i)
         return 0
 
     lax.fori_loop(0, GROUPS, backward, 0)
+    other = pl.multiple_of((1 - c) * PR, PR)
+    swap = remote(part.at[0, pl.ds(other, WINDOW)], own_in, own_s, own_r, sibling)
+    swap.start()
     for o in DONE[GROUPS - 1]:
         if not children(REDUCE, o):
             send_up(o)
@@ -417,43 +451,58 @@
                 rows = jnp.where(place < lens[k + 1], rows, 0.0)
             a_out[k] = rows.astype(BF16)
 
-    value = part[0]
+    swap.wait_recv()
+    first = pl.multiple_of(c * PR, PR)
+    window = pl.ds(first, WINDOW)
+    value = part[0, window] + own_in[...]
     for o in children(REDUCE, 0)[::-1]:
-        up(o).wait_recv()
-        value = value + rs_in[o].astype(F32)
-    fin[0, c] = value.astype(BF16)
+        for way in range(2):
+            for piece in range(2):
+                pl.when(c == piece)(lambda: up(o, piece, way).wait_recv())
+            value = value + rs_in[way, o, window].astype(F32)
+    factor = jnp.where(lax.broadcasted_iota(jnp.int32, (1, 256), 1) < 128, scaling, 1.0)
+    fin[0, c] = (value * factor).astype(BF16)
     finals = [
-        remote(fin.at[0, c], fin.at[0, c], fin_s.at[0], fin_r.at[0], sibling),
-        remote(fin.at[0, c], fin.at[1, c], fin_s.at[1], fin_r.at[1], across(2, c)),
-        remote(fin.at[0, c], fin.at[1, c], fin_s.at[2], fin_r.at[2], across(2, 1 - c)),
+        remote(fin.at[0, c], fin.at[0, c], fin_s.at[0], fin_r.at[0, 0], sibling),
+        remote(fin.at[0, c], fin.at[1, c], fin_s.at[1], fin_r.at[1, c], across(2, c)),
+        remote(fin.at[0, c], fin.at[1, c], fin_s.at[2], fin_r.at[1, c], across(2, 1 - c)),
     ]
     for f in finals[::-1]:
         f.start()
-    for f in finals:
-        f.wait_recv()
-    factor = jnp.where(lax.broadcasted_iota(jnp.int32, (1, 256), 1) < 128, scaling, 1.0)
     for h in range(2):
         half = hi if h == 0 else 1 - hi
-        value = ((fin[h, 0].astype(F32) + fin[h, 1].astype(F32)) * factor).astype(BF16)
-        pkvg[pl.ds(pl.multiple_of(half * PR, PR), PR)] = value[:PR]
-        for k in range(2):
-            akvg[k, pl.ds(pl.multiple_of(half * AR, AR), AR)] = value[
-                PR + k * AR : PR + (k + 1) * AR
-            ]
-
-    for copy in sends_q + sends_st + backs + finals:
+        if h == 0:
+            finals[0].wait_recv()
+        else:
+            for core in range(2):
+                block = fin.at[1, core]
+                pltpu.make_async_copy(block, block, fin_r.at[1, core]).wait()
+        pkvg[pl.ds(pl.multiple_of(half * PR, PR), PR)] = fin[h, 0, pl.ds(0, PR)]
+        for k in range(2):
+            akvg[k, pl.ds(pl.multiple_of(half * AR, AR), AR)] = fin[h, 1, pl.ds(k * AR, AR)]
+
+    for copy in sends_q + sends_st + backs + finals + [swap]:
         copy.wait_send()
     for o in GATHER:
-        def act(o=o):
-            hop(o).wait_send()
-            share(o).wait_send()
-            up(o).wait_send()
-
-        guard(o, act)
+        for piece in range(len(PARCELS)):
+            hop(o, piece).wait_send()
+            if o != 8:
+                share(o, piece).wait_send()
+
+        def sent(o=o):
+            for piece in range(2):
+                up(o, piece).wait_send()
+
+        guard(o, sent)
         if o == 8:
             pl.when(c == 1)(lambda: pass_on(8).wait_send())
         else:
             pass_on(o).wait_send()
+
+
+def place(*refs):
+    for source, target in zip(refs[:6], refs[6:]):
+        target[...] = source[...]
 
 
 def body(*args):
@@ -468,7 +517,7 @@
         jax.ShapeDtypeStruct((QP, 256), BF16),
         jax.ShapeDtypeStruct((2, QA, 256), BF16),
     )
-    return pl.pallas_call(
+    results = pl.pallas_call(
         kernel,
         out_shape=outs,
         in_specs=[hbm] * 6 + [pl.BlockSpec(memory_space=pltpu.SMEM)],
@@ -484,7 +533,7 @@
             pltpu.VMEM((GROUPS, 2, WIDTH * AR, NA), F32),
             pltpu.VMEM((GROUPS, 8, ROWS), F32),
             pltpu.VMEM((GROUPS, 128, ROWS), F32),
-            pltpu.VMEM((4, 8, ROWS), F32),
+            pltpu.VMEM((4, 3, 1, ROWS), F32),
             pltpu.VMEM((128, ROWS), F32),
             pltpu.VMEM((2, 4, OWN, 128), F32),
             pltpu.VMEM((2, 4, OWN, 128), BF16),
@@ -493,12 +542,13 @@
             pltpu.VMEM((9, BLOCK, 256), BF16),
             pltpu.VMEM((9, BLOCK, 256), BF16),
             pltpu.VMEM((9, BLOCK, 256), BF16),
-            pltpu.VMEM((9, BLOCK, 256), BF16),
-            pltpu.VMEM((2, 2, BLOCK, 256), BF16),
+            pltpu.VMEM((2, 9, BLOCK, 256), BF16),
+            pltpu.VMEM((2, 2, WINDOW, 256), BF16),
+            pltpu.VMEM((WINDOW, 256), F32),
             dma((9,)),
-            dma((16,)),
-            dma((9,)),
-            dma((9,)),
+            dma((len(PARCELS), 16)),
+            dma((len(PARCELS), 9)),
+            dma((len(PARCELS), 9)),
             dma((4,)),
             dma((4,)),
             dma((4,)),
@@ -507,15 +557,24 @@
             dma((2, 4)),
             dma((9,)),
             dma((9,)),
-            dma((9,)),
-            dma((9,)),
+            dma((2, 2, 9)),
+            dma((2, 9)),
+            dma((2, 2)),
             dma((3,)),
-            dma((3,)),
+            dma(()),
+            dma(()),
         ],
         compiler_params=pltpu.CompilerParams(
             collective_id=0, has_side_effects=True, vmem_limit_bytes=56 * 2**20
         ),
     )(*args)
+    return pl.pallas_call(
+        place,
+        out_shape=outs,
+        in_specs=[vmem] * 6,
+        out_specs=(vmem,) * 6,
+        compiler_params=pltpu.CompilerParams(vmem_limit_bytes=56 * 2**20),
+    )(*results)
 
 
 def solution(mesh):

time: 63.9 us -> 57.9 us (0.906)
  local copies, waits for them, and re-layouts: 4.82 us -> 0 us
  Pallas kernels: 57.9 us -> 57 us
    unnamed x16 -> x0, local copies, waits for them, and re-layouts: 4.82 us -> none
    pallas_call x1, Pallas kernels: 57.9 us -> 55.4 us  [body(): pl.pallas_call(kernel, out_shape=outs, in_specs=[hbm] * 6 + [pl.BlockSpec...]
    pallas_call x0 -> x1, Pallas kernels: none -> 1.63 us  [body(): pl.pallas_call(place, out_shape=outs, in_specs=[vmem] * 6, out_specs=(vme...]
where the time goes in v2:
time: 57.9 us; the launch traced here: 57.6 us
  Pallas kernels  57 us (98%)
  between operations  0.64 us (1%)
    pallas_call x1, Pallas kernels, body(): pl.pallas_call(kernel, out_shape=outs, in_specs=[hbm] * 6 + [pl.BlockSpec...  55.4 us
    pallas_call x1, Pallas kernels, body(): pl.pallas_call(place, out_shape=outs, in_specs=[vmem] * 6, out_specs=(vme...  1.63 us

profile of v2, /device:TPU:1, one launch (start us, length us, event | category | flops | bytes accessed | tf_op | source)
XLA Modules:
  0.0 57.6 jit_solution(16734648901730094878)
XLA Ops:
  0.6 55.4 %shard_map.118 = (bf16[96,128]{1,0:T(8,128)(2,1)}, bf16[2,64,128]{2,1,0:T(8,128)(2,1)}, bf16[96,128]{1,0:T(8,128)(2,1)}, bf16[2,64,128]{2,1,0:T(8,128)(2,1)}, bf...) custom-call(bf16[96,128]{1,0:T(8,128)(2,1)} %pq.1, bf16[2,64,128]{2,1,0:T(8,128)(2,1)} %aq.1, bf16[96,256]{1,0:T(8,128)(2,1)} %pkv.1, ...), custom_call_target="tpu_custom_call" | custom-call | tf_op jit(solution)/shard_map/pallas_call | solution.py:520
  56.0 1.6 %shard_map.119 = (bf16[96,128]{1,0:T(8,128)(2,1)}, bf16[2,64,128]{2,1,0:T(8,128)(2,1)}, bf16[96,128]{1,0:T(8,128)(2,1)}, bf16[2,64,128]{2,1,0:T(8,128)(2,1)}, bf...) custom-call(bf16[96,128]{1,0:T(8,128)(2,1)} %get-tuple-element.12.refs_0_, ...), custom_call_target="tpu_custom_call" | custom-call | tf_op jit(solution)/shard_map/pallas_call | solution.py:571

commit v3 on v2

--- a/solution.py
+++ b/solution.py
@@ -22,6 +22,7 @@
 NP, NA = 4 * QP, 4 * QA
 PARCELS = ((0, PR), (PR, 2 * AR))
 PIECES = ((0, PR), (PR, 2 * AR))
+FINISHER = (0, 1)
 WINDOW = 2 * AR
 GROUPS, WIDTH = 4, 4
 
@@ -48,6 +49,7 @@
 
 READY = [[o for o in GATHER if min(slot_of(o, 0), 15) // WIDTH == k] for k in range(GROUPS)]
 DONE = READY[::-1]
+TAKEN = [[], [2, 4], [5, 7], [8]]
 RELAYS = [o for o in ORDER if children(GATHER, o)]
 
 
@@ -65,7 +67,7 @@
 
 def kernel(
     pq, aq, pkv, akv, pg, ag, lens,
-    po, ao, pqg, aqg, pkvg, akvg,
+    packed,
     kv, qg, q_all, g_all, pp, dpp, pa, dpa, stat, ot, st, dqt, own_f, osend, orecv,
     part, sib_out, sib_in, rs_out, rs_in, fin, own_in,
     loc, kv_r, kv_s, kv_x, qg_r, qg_s, st_r, st_s, o_r, o_s, sib_r, sib_s, rs_r, rs_s, fin_r, fin_s, own_r, own_s,
@@ -110,14 +112,13 @@
         pairs.append((a_ref.at[0], qg.at[x, pl.ds(QP, QA), cols]))
         pairs.append((a_ref.at[1], qg.at[x, pl.ds(QP + QA, QA), cols]))
     loads = [pltpu.make_async_copy(a, b, loc.at[i]) for i, (a, b) in enumerate(pairs)]
-    for load in loads:
-        load.start()
-
     barrier = pltpu.get_barrier_semaphore()
     steps = sorted({o - p for o, p in GATHER.items()})
     senders = [ring(-s * d) for d in steps] + [across(d, c) for d in (1, 2, 3)] + [sibling]
     for device in senders:
         pl.semaphore_signal(barrier, inc=1, device_id=device, device_id_type=MESH)
+    for load in loads:
+        load.start()
     for load in loads:
         load.wait()
     pl.semaphore_wait(barrier, len(senders))
@@ -206,9 +207,8 @@
             @pl.when(g == k)
             def _(k=k):
                 if k:
-                    for o in READY[k]:
-                        if o not in RELAYS:
-                            arrive(o)
+                    for o in TAKEN[k]:
+                        arrive(o)
                 for o in READY[k]:
                     if o != 8:
                         theirs(o)
@@ -323,7 +323,7 @@
         rows = rows_of(piece)
         step = -s * (o - REDUCE[o])
         if REDUCE[o] == 0:
-            to = {"blk": lo * RING + lax.rem(z + step + 2 * RING, RING), "resp": hi * 2 + piece}
+            to = {"blk": lo * RING + lax.rem(z + step + 2 * RING, RING), "resp": hi * 2 + FINISHER[piece]}
         else:
             to = ring(step)
         way = c if direction is None else direction
@@ -335,7 +335,7 @@
         def act():
             pass_on(o).wait_recv()
             mine = slot_of(o, c)
-            for piece in range(2):
+            for piece in range(len(PIECES)):
                 rows = rows_of(piece)
                 value = part[mine, rows] + sib_in[o, rows].astype(F32)
                 for o2 in children(REDUCE, o):
@@ -431,25 +431,33 @@
             back.start()
             backs.append(back)
 
+    def early(o):
+        return lax.rem(z - s * o + RING, RING) < 7
+
     for o in sorted(REDUCE, reverse=True):
         if children(REDUCE, o):
-            send_up(o)
+            pl.when(early(o))(lambda o=o: send_up(o))
 
     for back in backs:
         back.wait_recv()
     place = blk * QA + lax.broadcasted_iota(jnp.int32, (QA, 128), 0)
-    for j, (p_out, a_out) in enumerate(((po, ao), (pqg, aqg))):
+    for j in range(2):
+        cols = pl.ds(128 * j, 128)
         value = own_f[j, x]
         for d in (1, 2, 3):
             value = value + orecv[j, d].astype(F32)
         if j:
             value = value * scaling
-        p_out[...] = value[:QP].astype(BF16)
+        packed[pl.ds(0, QP), cols] = value[:QP].astype(BF16)
         for k in range(2):
             rows = value[QP + k * QA : QP + (k + 1) * QA]
             if j == 0:
                 rows = jnp.where(place < lens[k + 1], rows, 0.0)
-            a_out[k] = rows.astype(BF16)
+            packed[pl.ds(QP + k * QA, QA), cols] = rows.astype(BF16)
+
+    for o in sorted(REDUCE, reverse=True):
+        if children(REDUCE, o):
+            pl.when(jnp.logical_not(early(o)))(lambda o=o: send_up(o))
 
     swap.wait_recv()
     first = pl.multiple_of(c * PR, PR)
@@ -457,8 +465,8 @@
     value = part[0, window] + own_in[...]
     for o in children(REDUCE, 0)[::-1]:
         for way in range(2):
-            for piece in range(2):
-                pl.when(c == piece)(lambda: up(o, piece, way).wait_recv())
+            for piece, core in enumerate(FINISHER):
+                pl.when(c == core)(lambda: up(o, piece, way).wait_recv())
             value = value + rs_in[way, o, window].astype(F32)
     factor = jnp.where(lax.broadcasted_iota(jnp.int32, (1, 256), 1) < 128, scaling, 1.0)
     fin[0, c] = (value * factor).astype(BF16)
@@ -477,9 +485,10 @@
             for core in range(2):
                 block = fin.at[1, core]
                 pltpu.make_async_copy(block, block, fin_r.at[1, core]).wait()
-        pkvg[pl.ds(pl.multiple_of(half * PR, PR), PR)] = fin[h, 0, pl.ds(0, PR)]
-        for k in range(2):
-            akvg[k, pl.ds(pl.multiple_of(half * AR, AR), AR)] = fin[h, 1, pl.ds(k * AR, AR)]
+        cols = pl.ds(256, 256)
+        packed[pl.ds(pl.multiple_of(half * PR, PR), PR), cols] = fin[h, 0, pl.ds(0, PR)]
+        for k in range(2):
+            packed[pl.ds(pl.multiple_of(QP + k * QA + half * AR, AR), AR), cols] = fin[h, 1, pl.ds(k * AR, AR)]
 
     for copy in sends_q + sends_st + backs + finals + [swap]:
         copy.wait_send()
@@ -490,7 +499,7 @@
                 share(o, piece).wait_send()
 
         def sent(o=o):
-            for piece in range(2):
+            for piece in range(len(PIECES)):
                 up(o, piece).wait_send()
 
         guard(o, sent)
@@ -500,9 +509,12 @@
             pass_on(o).wait_send()
 
 
-def place(*refs):
-    for source, target in zip(refs[:6], refs[6:]):
-        target[...] = source[...]
+def place(packed, *refs):
+    for j in range(3):
+        cols = pl.ds(128 * j, 128 if j < 2 else 256)
+        refs[2 * j][...] = packed[pl.ds(0, QP), cols]
+        for k in range(2):
+            refs[2 * j + 1][k] = packed[pl.ds(QP + k * QA, QA), cols]
 
 
 def body(*args):
@@ -519,9 +531,9 @@
     )
     results = pl.pallas_call(
         kernel,
-        out_shape=outs,
+        out_shape=jax.ShapeDtypeStruct((OWN, 512), BF16),
         in_specs=[hbm] * 6 + [pl.BlockSpec(memory_space=pltpu.SMEM)],
-        out_specs=(vmem,) * 6,
+        out_specs=vmem,
         scratch_shapes=[
             pltpu.VMEM((16, BLOCK, 256), BF16),
             pltpu.VMEM((4, OWN, 256), BF16),
@@ -557,8 +569,8 @@
             dma((2, 4)),
             dma((9,)),
             dma((9,)),
-            dma((2, 2, 9)),
-            dma((2, 9)),
+            dma((2, len(PIECES), 9)),
+            dma((len(PIECES), 9)),
             dma((2, 2)),
             dma((3,)),
             dma(()),
@@ -571,10 +583,10 @@
     return pl.pallas_call(
         place,
         out_shape=outs,
-        in_specs=[vmem] * 6,
+        in_specs=[vmem],
         out_specs=(vmem,) * 6,
         compiler_params=pltpu.CompilerParams(vmem_limit_bytes=56 * 2**20),
-    )(*results)
+    )(results)
 
 
 def solution(mesh):

time: 57.9 us -> 56.3 us (0.972)
  Pallas kernels: 57 us -> 55.4 us
    pallas_call x2, Pallas kernels: 57 us -> 55.4 us  [the longest x1 53.7 us: body(): pl.pallas_call(kernel, out_shape=jax.ShapeDtypeStruct((OWN, 512), BF16),...]
where the time goes in v3:
time: 56.3 us; the launch traced here: 56 us
  Pallas kernels  55.4 us (98%)
  between operations  0.64 us (1%)
    pallas_call x1, Pallas kernels, body(): pl.pallas_call(kernel, out_shape=jax.ShapeDtypeStruct((OWN, 512), BF16),...  53.7 us
    pallas_call x1, Pallas kernels, body(): pl.pallas_call(place, out_shape=outs, in_specs=[vmem], out_specs=(vmem,)...  1.65 us

profile of v3, /device:TPU:1, one launch (start us, length us, event | category | flops | bytes accessed | tf_op | source)
XLA Modules:
  0.0 56.0 jit_solution(5432393409910502845)
XLA Ops:
  0.6 53.7 %shard_map.118.packed = bf16[224,512]{1,0:T(8,128)(2,1)} custom-call(bf16[96,128]{1,0:T(8,128)(2,1)} %pq.1, bf16[2,64,128]{2,1,0:T(8,128)(2,1)} %aq.1, bf16[96,256]{1,0:T(8,128)(2,1)} %pkv.1, bf16[2,64,256]{2,1,0:T(8,128)(2,1)} %akv.1, bf16[96,128]{1,0:T(8,128)(2,1)} %pg.1, bf16[2,64,128]{2,1,0:T(8,128)(2,1)} %ag.1, s32[3]{0:T(128)} %lens.1), custom_call_target="tpu_custom_call" | custom-call | tf_op jit(solution)/shard_map/pallas_call | solution.py:532
  54.4 1.6 %shard_map.119 = (bf16[96,128]{1,0:T(8,128)(2,1)}, bf16[2,64,128]{2,1,0:T(8,128)(2,1)}, bf16[96,128]{1,0:T(8,128)(2,1)}, bf16[2,64,128]{2,1,0:T(8,128)(2,1)}, bf...) custom-call(bf16[224,512]{1,0:T(8,128)(2,1)} %shard_map.118.packed), custom_call_target="tpu_custom_call" | custom-call | tf_op jit(solution)/shard_map/pallas_call | solution.py:583

commit v4 on v3

--- a/solution.py
+++ b/solution.py
@@ -49,7 +49,7 @@
 
 READY = [[o for o in GATHER if min(slot_of(o, 0), 15) // WIDTH == k] for k in range(GROUPS)]
 DONE = READY[::-1]
-TAKEN = [[], [2, 4], [5, 7], [8]]
+TAKEN = [[3, 1, 6, 2, 4], [], [5, 7], [8]]
 RELAYS = [o for o in ORDER if children(GATHER, o)]
 
 
@@ -160,11 +160,8 @@
     for piece in range(len(PARCELS)):
         for o in children(GATHER, 0):
             hop(o, piece).start()
-    for o in RELAYS:
+    for o in TAKEN[0]:
         arrive(o)
-    for o in READY[0]:
-        if o not in RELAYS:
-            arrive(o)
     for copy in sends_q:
         copy.wait_recv()
 

time: 56.3 us -> 55 us (0.977); the launches traced: 56 us -> 54.1 us
  Pallas kernels: 55.4 us -> 53.5 us
    pallas_call x1, Pallas kernels: 53.7 us -> 51.8 us  [body(): pl.pallas_call(kernel, out_shape=jax.ShapeDtypeStruct((OWN, 512), BF16),...]
where the time goes in v4:
time: 55 us; the launch traced here: 54.1 us
  Pallas kernels  53.5 us (97%)
  between operations  0.64 us (1%)
    pallas_call x1, Pallas kernels, body(): pl.pallas_call(kernel, out_shape=jax.ShapeDtypeStruct((OWN, 512), BF16),...  51.8 us
    pallas_call x1, Pallas kernels, body(): pl.pallas_call(place, out_shape=outs, in_specs=[vmem], out_specs=(vmem,)...  1.65 us

profile of v4, /device:TPU:1, one launch (start us, length us, event | category | flops | bytes accessed | tf_op | source)
XLA Modules:
  0.0 54.1 jit_solution(2628311990654927606)
XLA Ops:
  0.6 51.8 %shard_map.118.packed = bf16[224,512]{1,0:T(8,128)(2,1)} custom-call(bf16[96,128]{1,0:T(8,128)(2,1)} %pq.1, bf16[2,64,128]{2,1,0:T(8,128)(2,1)} %aq.1, bf16[96,256]{1,0:T(8,128)(2,1)} %pkv.1, bf16[2,64,256]{2,1,0:T(8,128)(2,1)} %akv.1, bf16[96,128]{1,0:T(8,128)(2,1)} %pg.1, bf16[2,64,128]{2,1,0:T(8,128)(2,1)} %ag.1, s32[3]{0:T(128)} %lens.1), custom_call_target="tpu_custom_call" | custom-call | tf_op jit(solution)/shard_map/pallas_call | solution.py:529
  52.5 1.6 %shard_map.119 = (bf16[96,128]{1,0:T(8,128)(2,1)}, bf16[2,64,128]{2,1,0:T(8,128)(2,1)}, bf16[96,128]{1,0:T(8,128)(2,1)}, bf16[2,64,128]{2,1,0:T(8,128)(2,1)}, bf...) custom-call(bf16[224,512]{1,0:T(8,128)(2,1)} %shard_map.118.packed), custom_call_target="tpu_custom_call" | custom-call | tf_op jit(solution)/shard_map/pallas_call | solution.py:580

commit v5 on v4

--- a/solution.py
+++ b/solution.py
@@ -251,8 +251,7 @@
         dpp[g] = dp
         total = jnp.sum(wp, axis=0, keepdims=True)
         delta = jnp.sum(wp * dp, axis=0, keepdims=True)
-        out = dot_first(values, wp.astype(BF16))
-        totals, deltas, outs = [total[:, :NP]], [delta[:, :NP]], [out[:, :NP]]
+        totals, deltas = [total[:, :NP]], [delta[:, :NP]]
         for k in range(2):
             a, b = NP + k * NA, NP + (k + 1) * NA
             wa = jnp.exp(sa[k] - top[:, a:b])
@@ -261,11 +260,9 @@
             dpa[g, k] = da
             totals.append(total[:, a:b] + jnp.sum(wa, axis=0, keepdims=True))
             deltas.append(delta[:, a:b] + jnp.sum(wa * da, axis=0, keepdims=True))
-            outs.append(out[:, a:b] + dot_first(kinds[k][:, 128:], wa.astype(BF16)))
         stat[g, pl.ds(0, 1)] = top
         stat[g, pl.ds(1, 1)] = jnp.concatenate(totals, axis=1)
         stat[g, pl.ds(2, 1)] = jnp.concatenate(deltas, axis=1)
-        ot[g] = jnp.concatenate(outs, axis=1)
 
     def forward(g, _):
         receive(g)
@@ -281,7 +278,7 @@
         delta = sum(f * p[2] for f, p in zip(factors, parts))
         return top, total, delta, factors
 
-    top, total, delta, factors = merge(
+    top, total, delta, _ = merge(
         [[stat[i, pl.ds(k, 1)] for k in range(3)] for i in range(GROUPS)]
     )
     st[0, 0] = top
@@ -292,13 +289,12 @@
     ]
     for d in (1, 0, 2):
         sends_st[d].start()
-    ot[0] = sum(f * ot[i] for i, f in enumerate(factors))
     dqt[...] = jnp.zeros_like(dqt)
+    ot[...] = jnp.zeros_like(ot)
     for copy in sends_st:
         copy.wait_recv()
     all_top, total, delta, _ = merge([[st[d, k] for k in range(3)] for d in range(4)])
     delta = delta / total
-    scale_own = jnp.exp(top - all_top) / total
     for i in range(GROUPS):
         stat[i, pl.ds(3, 1)] = jnp.exp(stat[i, pl.ds(0, 1)] - all_top) / total
 
@@ -356,32 +352,37 @@
     def differentiate(g):
         base = g * WIDTH
         rows_p = kind_rows(kv, base, 0)
-        keys = rows_p[:, :128]
+        keys, values = rows_p[:, :128], rows_p[:, 128:]
         factor = stat[g, pl.ds(3, 1)]
         w = pp[g] * factor
+        wb = w.astype(BF16)
         ds = (w * (dpp[g] - delta)).astype(BF16)
         part[pl.ds(base, WIDTH), pl.ds(0, PR), pl.ds(0, 128)] = dot(ds, q_all[...]).reshape(
             WIDTH, PR, 128
         )
         part[pl.ds(base, WIDTH), pl.ds(0, PR), pl.ds(128, 128)] = dot(
-            w.astype(BF16), g_all[...]
+            wb, g_all[...]
         ).reshape(WIDTH, PR, 128)
         dq = dot_first(keys, ds)
-        dqs = [dq[:, :NP]]
+        out = dot_first(values, wb)
+        dqs, outs = [dq[:, :NP]], [out[:, :NP]]
         for k in range(2):
             a, b = NP + k * NA, NP + (k + 1) * NA
             rows_a = kind_rows(kv, base, k + 1)
             w = pa[g, k] * factor[:, a:b]
+            wb = w.astype(BF16)
             ds = (w * (dpa[g, k] - delta[:, a:b])).astype(BF16)
             where = pl.ds(PR + k * AR, AR)
             part[pl.ds(base, WIDTH), where, pl.ds(0, 128)] = dot(
                 ds, q_all[pl.ds(a, NA)]
             ).reshape(WIDTH, AR, 128)
             part[pl.ds(base, WIDTH), where, pl.ds(128, 128)] = dot(
-                w.astype(BF16), g_all[pl.ds(a, NA)]
+                wb, g_all[pl.ds(a, NA)]
             ).reshape(WIDTH, AR, 128)
             dqs.append(dq[:, a:b] + dot_first(rows_a[:, :128], ds))
+            outs.append(out[:, a:b] + dot_first(rows_a[:, 128:], wb))
         dqt[...] += jnp.concatenate(dqs, axis=1)
+        ot[...] += jnp.concatenate(outs, axis=1)
 
     def reduce(i):
         for k in range(GROUPS):
@@ -409,7 +410,7 @@
             send_up(o)
 
     backs = []
-    for j, whole in enumerate((ot[0] * scale_own, dqt[...])):
+    for j, whole in enumerate((ot[...], dqt[...])):
         rows = whole.T
         for d in range(4):
             for start, count, at in (
@@ -541,7 +542,7 @@
             pltpu.VMEM((GROUPS, 2, WIDTH * AR, NA), F32),
             pltpu.VMEM((GROUPS, 2, WIDTH * AR, NA), F32),
             pltpu.VMEM((GROUPS, 8, ROWS), F32),
-            pltpu.VMEM((GROUPS, 128, ROWS), F32),
+            pltpu.VMEM((128, ROWS), F32),
             pltpu.VMEM((4, 3, 1, ROWS), F32),
             pltpu.VMEM((128, ROWS), F32),
             pltpu.VMEM((2, 4, OWN, 128), F32),

time: 55 us -> 53.9 us (0.980)
  Pallas kernels: 53.5 us -> 52.9 us
    pallas_call x1, Pallas kernels: 51.8 us -> 51.3 us  [body(): pl.pallas_call(kernel, out_shape=jax.ShapeDtypeStruct((OWN, 512), BF16),...]
where the time goes in v5:
time: 53.9 us; the launch traced here: 53.6 us
  Pallas kernels  52.9 us (98%)
  between operations  0.64 us (1%)
    pallas_call x1, Pallas kernels, body(): pl.pallas_call(kernel, out_shape=jax.ShapeDtypeStruct((OWN, 512), BF16),...  51.3 us
    pallas_call x1, Pallas kernels, body(): pl.pallas_call(place, out_shape=outs, in_specs=[vmem], out_specs=(vmem,)...  1.65 us

profile of v5, /device:TPU:1, one launch (start us, length us, event | category | flops | bytes accessed | tf_op | source)
XLA Modules:
  0.0 53.6 jit_solution(923166756305654904)
XLA Ops:
  0.6 51.3 %shard_map.118.packed = bf16[224,512]{1,0:T(8,128)(2,1)} custom-call(bf16[96,128]{1,0:T(8,128)(2,1)} %pq.1, bf16[2,64,128]{2,1,0:T(8,128)(2,1)} %aq.1, bf16[96,256]{1,0:T(8,128)(2,1)} %pkv.1, bf16[2,64,256]{2,1,0:T(8,128)(2,1)} %akv.1, bf16[96,128]{1,0:T(8,128)(2,1)} %pg.1, bf16[2,64,128]{2,1,0:T(8,128)(2,1)} %ag.1, s32[3]{0:T(128)} %lens.1), custom_call_target="tpu_custom_call" | custom-call | tf_op jit(solution)/shard_map/pallas_call | solution.py:530
  51.9 1.6 %shard_map.119 = (bf16[96,128]{1,0:T(8,128)(2,1)}, bf16[2,64,128]{2,1,0:T(8,128)(2,1)}, bf16[96,128]{1,0:T(8,128)(2,1)}, bf16[2,64,128]{2,1,0:T(8,128)(2,1)}, bf...) custom-call(bf16[224,512]{1,0:T(8,128)(2,1)} %shard_map.118.packed), custom_call_target="tpu_custom_call" | custom-call | tf_op jit(solution)/shard_map/pallas_call | solution.py:581

commit v6 on v5

--- a/solution.py
+++ b/solution.py
@@ -162,6 +162,8 @@
             hop(o, piece).start()
     for o in TAKEN[0]:
         arrive(o)
+    dqt[...] = jnp.zeros_like(dqt)
+    ot[...] = jnp.zeros_like(ot)
     for copy in sends_q:
         copy.wait_recv()
 
@@ -289,8 +291,6 @@
     ]
     for d in (1, 0, 2):
         sends_st[d].start()
-    dqt[...] = jnp.zeros_like(dqt)
-    ot[...] = jnp.zeros_like(ot)
     for copy in sends_st:
         copy.wait_recv()
     all_top, total, delta, _ = merge([[st[d, k] for k in range(3)] for d in range(4)])

time: 53.9 us -> 53.9 us (level)
  no operation moved by 1% of the time
where the time goes in v6:
time: 53.9 us; the launch traced here: 53.6 us
  Pallas kernels  52.9 us (98%)
  between operations  0.64 us (1%)
    pallas_call x1, Pallas kernels, body(): pl.pallas_call(kernel, out_shape=jax.ShapeDtypeStruct((OWN, 512), BF16),...  51.3 us
    pallas_call x1, Pallas kernels, body(): pl.pallas_call(place, out_shape=outs, in_specs=[vmem], out_specs=(vmem,)...  1.65 us

profile of v6, /device:TPU:1, one launch (start us, length us, event | category | flops | bytes accessed | tf_op | source)
XLA Modules:
  0.0 53.6 jit_solution(10656168753936999195)
XLA Ops:
  0.6 51.3 %shard_map.118.packed = bf16[224,512]{1,0:T(8,128)(2,1)} custom-call(bf16[96,128]{1,0:T(8,128)(2,1)} %pq.1, bf16[2,64,128]{2,1,0:T(8,128)(2,1)} %aq.1, bf16[96,256]{1,0:T(8,128)(2,1)} %pkv.1, bf16[2,64,256]{2,1,0:T(8,128)(2,1)} %akv.1, bf16[96,128]{1,0:T(8,128)(2,1)} %pg.1, bf16[2,64,128]{2,1,0:T(8,128)(2,1)} %ag.1, s32[3]{0:T(128)} %lens.1), custom_call_target="tpu_custom_call" | custom-call | tf_op jit(solution)/shard_map/pallas_call | solution.py:530
  51.9 1.6 %shard_map.119 = (bf16[96,128]{1,0:T(8,128)(2,1)}, bf16[2,64,128]{2,1,0:T(8,128)(2,1)}, bf16[96,128]{1,0:T(8,128)(2,1)}, bf16[2,64,128]{2,1,0:T(8,128)(2,1)}, bf...) custom-call(bf16[224,512]{1,0:T(8,128)(2,1)} %shard_map.118.packed), custom_call_target="tpu_custom_call" | custom-call | tf_op jit(solution)/shard_map/pallas_call | solution.py:581
